TPU v7x, 128 devices: a whole 4x4x4 slice. The times are simulated.
128 devices in a mesh: dp: 16 (over y_lo, z, core), mp: 8 (over y_hi, x).
Axes of the slice: x: 4, y: 4 (y_hi: 2, y_lo: 2; y = y_hi * 2 + y_lo), z: 4, core: 2. Of those that a mesh axis runs over, the one named last changes fastest.
Arguments:
- states: bfloat16 [16, 1024, 3072], P('dp', 'mp'), may hold values from -6 to 6
- adjoint: bfloat16 [16, 1024, 3072], P('dp', 'mp'), may hold values from -6 to 6
- step_index: int32 [16], P('dp'), may hold values from 0 to 27
- modulation: float32 [28, 3, 3072], replicated, may hold values from -3 to 3
- up_projection_weight: bfloat16 [3072, 6144], P(None, 'mp'), may hold values from -0.109375 to 0.109375
- down_projection_weight: bfloat16 [6144, 3072], P('mp'), may hold values from -0.078125 to 0.078125
- offset: bfloat16 [3072, 6144], P('dp', 'mp'), may hold values from -0.078125 to 0.078125
Outputs:
- adjoint_rate: float32 [16, 1024, 3072], P('dp', 'mp')
- offset_grad: float32 [3072, 6144], P('dp', 'mp')
All inputs are finite; a program needn't handle non-finite values.
Results may differ from a plain program's by a relative error of at most 0.019.
Values may be sent and summed in bfloat16 or wider, within the bound.
A program may use at most 128 MiB of HBM per device.

v0:
```python
import math

import jax
import jax.numpy as jnp
from jax import lax
from jax.sharding import PartitionSpec as P


def gelu_tanh(value):
    coeff = math.sqrt(2.0 / math.pi)
    inner = coeff * (value + 0.044715 * value * value * value)
    return 0.5 * value * (1.0 + jnp.tanh(inner))


def gelu_slope(value):
    coeff = math.sqrt(2.0 / math.pi)
    inner = coeff * (value + 0.044715 * value * value * value)
    tangent = jnp.tanh(inner)
    return 0.5 * (1.0 + tangent) + 0.5 * value * (1.0 - tangent * tangent) * coeff * (
        1.0 + 3.0 * 0.044715 * value * value
    )


def per_device(
    states, adjoint, step_index, modulation, up_projection_weight, down_projection_weight, offset
):
    tok_rows = states.shape[1]
    step_count = modulation.shape[0]
    onehot = (step_index[:, None] == jnp.arange(step_count, dtype=jnp.int32)[None, :]).astype(
        jnp.float32
    )
    mods = jnp.einsum("sk,kcd->scd", onehot, modulation, precision=lax.Precision.HIGHEST)
    shift = mods[:, 0][:, None, :]
    scale = mods[:, 1][:, None, :]
    gate = mods[:, 2][:, None, :]
    timing = (step_index.astype(jnp.float32) + 1.0) / (step_count + 1.0)
    sigma = jnp.sqrt(2.0 * (1.0 - timing) / timing)[:, None, None]
    whole, adj_whole = (
        lax.all_gather(states, "mp", axis=1, tiled=True),
        lax.all_gather(adjoint, "mp", axis=1, tiled=True),
    )
    inputs = whole.astype(jnp.float32)
    mean = jnp.mean(inputs, axis=-1, keepdims=True)
    var = jnp.mean((inputs - mean) ** 2, axis=-1, keepdims=True)
    rstd = lax.rsqrt(var + 1e-06)
    normed = (inputs - mean) * rstd
    modulated_input = (normed * (1.0 + scale) + shift).astype(jnp.bfloat16)
    hidden_features = jnp.einsum(
        "izq,qm->izm", modulated_input, up_projection_weight, preferred_element_type=jnp.float32
    )
    activation_output = gelu_tanh(hidden_features).astype(jnp.bfloat16)
    gated_output = (adj_whole.astype(jnp.float32) * gate).astype(jnp.bfloat16)
    activation_gradient = jnp.einsum(
        "wni,qi->wnq", gated_output, down_projection_weight, preferred_element_type=jnp.float32
    )
    hidden_gradient = (activation_gradient * gelu_slope(hidden_features)).astype(jnp.bfloat16)
    vector_jacobian_share = jnp.einsum(
        "ceu,nu->cen", hidden_gradient, up_projection_weight, preferred_element_type=jnp.float32
    )
    velocity_part = jnp.einsum(
        "ceu,nu->cen",
        activation_output,
        lax.all_gather(offset, "dp", axis=0, tiled=True),
        preferred_element_type=jnp.float32,
    )
    grad_mod, velocity_gap = (
        lax.psum_scatter(
            vector_jacobian_share.astype(jnp.bfloat16), "mp", scatter_dimension=1, tiled=True
        ).astype(jnp.float32),
        lax.psum_scatter(
            velocity_part.astype(jnp.bfloat16), "mp", scatter_dimension=1, tiled=True
        ).astype(jnp.float32),
    )
    first = lax.axis_index("mp") * tok_rows
    normed_local = lax.dynamic_slice_in_dim(normed, first, tok_rows, 1)
    rstd_local = lax.dynamic_slice_in_dim(rstd, first, tok_rows, 1)
    scaled = grad_mod * (1.0 + scale)
    adjoint_rate = rstd_local * (
        scaled
        - jnp.mean(scaled, axis=-1, keepdims=True)
        - normed_local * jnp.mean(scaled * normed_local, axis=-1, keepdims=True)
    )
    adj_local = adjoint.astype(jnp.float32)
    residual = 2.0 / sigma * gate * velocity_gap + sigma * adj_local
    weighted = (gate / sigma * residual).astype(jnp.bfloat16)
    weighted_total = lax.all_gather(weighted, "mp", axis=1, tiled=True)
    total_rows = lax.axis_size("dp") * states.shape[0] * lax.axis_size("mp") * tok_rows
    multiplier_term = 1.0 / math.sqrt(total_rows)
    offset_grad = lax.psum_scatter(
        (
            jnp.einsum(
                "vzc,vza->ca", weighted_total, activation_output, preferred_element_type=jnp.float32
            )
            * multiplier_term
        ).astype(jnp.bfloat16),
        "dp",
        scatter_dimension=0,
        tiled=True,
    ).astype(jnp.float32)
    return (adjoint_rate, offset_grad)


def solution(mesh):
    in_specs = (
        P("dp", "mp", None),
        P("dp", "mp", None),
        P("dp"),
        P(),
        P(None, "mp"),
        P("mp", None),
        P("dp", "mp"),
    )
    out_specs = (P("dp", "mp", None), P("dp", "mp"))
    return jax.shard_map(
        per_device, mesh=mesh, in_specs=in_specs, out_specs=out_specs, check_vma=False
    )
```

profile of v0, /device:TPU:1, one launch (start us, length us, event | category | flops | bytes accessed | tf_op | source)
XLA Modules:
  0.0 606.8 jit_solution(3786703231264151787)
XLA Ops:
  7.2 0.0 copy-start
  7.2 0.0 all-gather.5.cloned.1.call-start
  7.2 0.7 all-gather.5.cloned.1.call-update
  7.9 0.0 all-gather.9.cloned.1.call-start
  8.0 0.7 all-gather.9.cloned.1.call-update
  8.7 0.0 reduce-scatter.6.cloned.1.call-start
  9.5 0.0 copy-done
  9.5 0.5 fusion.27
  10.1 92.7 %all-gather.5.cloned.1.call-done = bf16[1,1024,3072]{2,1,0:T(8,128)(2,1)} async-done(((bf16[1,128,3072]{2,1,0:T(8,128)(2,1)}), bf16[1,1024,3072]{2,1,0:T(8,128)(2,1)}) %all-gather.5.cloned.1.call-update) | async-done | bytes 6291472 | tf_op jit(solution)/shard_map/all_gather | solution.py:39
  102.8 0.0 copy-start.2
  102.8 3.8 convert_reduce_fusion
  106.6 0.8 copy-done.2
  107.4 0.0 copy-start.4
  107.4 1.8 fusion.2
  109.1 0.6 copy-done.4
  109.7 7.4 %fusion.7 = f32[1024,768]{1,0:T(8,128)} fusion(bf16[3072,768]{1,0:T(8,128)(2,1)S(1)} %copy-done.4, f32[3072]{0:T(1024)S(1)} %bitcast.60, f32[3072]{0:T(1024)S(1)} %bitcast.54, bf16[1,1024,3072]{2,1,0:T(8,128)(2,1)S(1)} %copy-done.2, f32[1024]{0:T(1024)S(1)} %add_rsqrt_fusion, f32[1024]{0:T(1024)S(1)} %broadcast_multiply_fusion), kind=kOutput, calls=%fused_computation.11 | convolution fusion | flops 4850712576 | bytes 14188544 | tf_op jit(solution)/shard_map/izq,qm->izm/dot_general | solution.py:48
  117.1 24.8 %all-gather.9.cloned.1.call-done = bf16[3072,768]{1,0:T(8,128)(2,1)} async-done(((bf16[192,768]{1,0:T(8,128)(2,1)}), bf16[3072,768]{1,0:T(8,128)(2,1)}) %all-gather.9.cloned.1.call-update) | async-done | bytes 4718608 | tf_op jit(solution)/shard_map/all_gather | solution.py:63
  141.9 9.9 %convert_bitcast_fusion = bf16[1,1024,3072]{2,1,0:T(8,128)(2,1)} fusion(bf16[3072,768]{1,0:T(8,128)(2,1)} %all-gather.9.cloned.1.call-done, f32[1024,768]{1,0:T(8,128)} %fusion.7), kind=kOutput, calls=%fused_computation.14 | convolution fusion | flops 4842061824 | bytes 14155776 | tf_op jit(solution)/shard_map/ceu,nu->cen/dot_general | solution.py:60
  151.8 0.0 copy-start.3
  151.8 0.0 reduce-scatter.6.cloned.1.call-update
  151.9 0.0 all-gather.7.cloned.1.call-start
  151.9 0.5 all-gather.7.cloned.1.call-update
  152.4 0.0 all-gather.11.cloned.1.call-start
  152.5 97.4 %reduce-scatter.6.cloned.1.call-done = bf16[1,128,3072]{2,1,0:T(8,128)(2,1)} async-done(((bf16[1,1024,3072]{2,1,0:T(8,128)(2,1)}), bf16[1,128,3072]{2,1,0:T(8,128)(2,1)}) %reduce-scatter.6.cloned.1.call-update) | async-done | bytes 786448 | tf_op jit(solution)/shard_map/reduce_scatter | solution.py:70
  249.9 0.0 copy-done.3
  249.9 2.3 multiply_convert_fusion.3
  252.3 0.0 all-gather.11.cloned.1.call-update
  252.3 0.2 reduce-scatter.4.cloned.1.call-start
  252.5 88.2 %all-gather.7.cloned.1.call-done = bf16[1,1024,3072]{2,1,0:T(8,128)(2,1)} async-done(((bf16[1,128,3072]{2,1,0:T(8,128)(2,1)}), bf16[1,1024,3072]{2,1,0:T(8,128)(2,1)}) %all-gather.7.cloned.1.call-update) | async-done | bytes 6291472 | tf_op jit(solution)/shard_map/all_gather | solution.py:40
  340.8 20.9 %convert_bitcast_fusion.1 = bf16[1,1024,3072]{2,1,0:T(8,128)(2,1)} fusion(bf16[3072,768]{1,0:T(8,128)(2,1)} %param.11, f32[1024,768]{1,0:T(8,128)} %fusion.7, bf16[768,3072]{1,0:T(8,128)(2,1)} %param.12, bf16[1,1024,3072]{2,1,0:T(8,128)(2,1)} %all-gather.7.cloned.1.call-done, f32[3072]{0:T(1024)S(1)} %bitcast.59), kind=kOutput, calls=%fused_computation.15 | convolution fusion | flops 9691201536 | bytes 25178112 | tf_op jit(solution)/shard_map/ceu,nu->cen/dot_general | solution.py:57
  361.6 0.0 reduce-scatter.4.cloned.1.call-update
  361.6 0.0 reduce-scatter.8.cloned.1.call-start
  361.7 69.6 %all-gather.11.cloned.1.call-done = bf16[1,1024,3072]{2,1,0:T(8,128)(2,1)} async-done(((bf16[1,128,3072]{2,1,0:T(8,128)(2,1)}), bf16[1,1024,3072]{2,1,0:T(8,128)(2,1)}) %all-gather.11.cloned.1.call-update) | async-done | bytes 6291472 | tf_op jit(solution)/shard_map/all_gather | solution.py:86
  431.3 9.9 %multiply_convert_fusion.1 = bf16[3072,768]{1,0:T(8,128)(2,1)} fusion(bf16[1,1024,3072]{2,1,0:T(8,128)(2,1)} %all-gather.11.cloned.1.call-done, f32[1024,768]{1,0:T(8,128)} %fusion.7), kind=kOutput, calls=%fused_computation.7 | convolution fusion | flops 4843634688 | bytes 14155776 | tf_op jit(solution)/shard_map/vzc,vza->ca/dot_general | solution.py:91
  441.2 0.0 reduce-scatter.8.cloned.1.call-update
  441.3 0.1 dynamic_slice.6
  441.3 0.0 copy-start.1
  441.3 10.6 %fusion = f32[1,1024,3072]{2,1,0:T(8,128)} fusion(bf16[1,1024,3072]{2,1,0:T(8,128)(2,1)} %all-gather.5.cloned.1.call-done, f32[1024]{0:T(1024)S(1)} %add_rsqrt_fusion, f32[1024]{0:T(1024)S(1)} %broadcast_multiply_fusion), kind=kLoop, calls=%fused_computation.2 | loop fusion | flops 9437184 | bytes 18882560 | tf_op jit(solution)/shard_map/mul | solution.py:46
  451.9 80.5 %reduce-scatter.4.cloned.1.call-done = bf16[1,128,3072]{2,1,0:T(8,128)(2,1)} async-done(((bf16[1,1024,3072]{2,1,0:T(8,128)(2,1)}), bf16[1,128,3072]{2,1,0:T(8,128)(2,1)}) %reduce-scatter.4.cloned.1.call-update) | async-done | bytes 786448 | tf_op jit(solution)/shard_map/reduce_scatter | solution.py:67
  532.4 2.0 fusion.25
  534.4 3.2 subtract_multiply_fusion
  537.6 60.5 %reduce-scatter.8.cloned.1.call-done = bf16[192,768]{1,0:T(8,128)(2,1)} async-done(((bf16[3072,768]{1,0:T(8,128)(2,1)}), bf16[192,768]{1,0:T(8,128)(2,1)}) %reduce-scatter.8.cloned.1.call-update) | async-done | bytes 294928 | tf_op jit(solution)/shard_map/reduce_scatter | solution.py:89
  598.1 1.8 convert_element_type.70
  599.9 0.0 copy-done.1
  (5 shorter events, 0.1 us)
Async XLA Ops:
  7.2 2.3 copy-start
  7.2 95.6 %all-gather.5.cloned.1.call-start = ((), (), s32[]{:S(2)}) async-start(), calls=%async_computation.3 | async-start | bytes 7077888 | tf_op jit(solution)/shard_map/all_gather | solution.py:39
  7.9 134.0 %all-gather.9.cloned.1.call-start = ((), (), s32[]{:S(2)}) async-start(), calls=%async_computation.6 | async-start | bytes 5013504 | tf_op jit(solution)/shard_map/all_gather | solution.py:63
  8.7 241.3 %reduce-scatter.6.cloned.1.call-start = ((), (), s32[]{:S(2)}) async-start(), calls=%async_computation.7 | async-start | bytes 7077888 | tf_op jit(solution)/shard_map/reduce_scatter | solution.py:70
  102.8 4.6 copy-start.2
  107.4 2.3 copy-start.4
  151.8 98.1 %copy-start.3 = (bf16[1,128,3072]{2,1,0:T(8,128)(2,1)S(1)}, bf16[1,128,3072]{2,1,0:T(8,128)(2,1)}, u32[]{:S(2)}) copy-start(bf16[1,128,3072]{2,1,0:T(8,128)(2,1)} %param.8) | copy-start | bytes 2359300
  151.9 188.9 %all-gather.7.cloned.1.call-start = ((), (), s32[]{:S(2)}) async-start(), calls=%async_computation.4 | async-start | bytes 7077888 | tf_op jit(solution)/shard_map/all_gather | solution.py:40
  152.4 278.9 %all-gather.11.cloned.1.call-start = ((), (), s32[]{:S(2)}) async-start(), calls=%async_computation.8 | async-start | bytes 7077888 | tf_op jit(solution)/shard_map/all_gather | solution.py:86
  252.3 280.1 %reduce-scatter.4.cloned.1.call-start = ((), (), s32[]{:S(2)}) async-start(), calls=%async_computation.5 | async-start | bytes 7077888 | tf_op jit(solution)/shard_map/reduce_scatter | solution.py:67
  361.6 236.5 %reduce-scatter.8.cloned.1.call-start = ((), (), s32[]{:S(2)}) async-start(), calls=%async_computation.9 | async-start | bytes 5013504 | tf_op jit(solution)/shard_map/reduce_scatter | solution.py:89
  441.3 158.6 %copy-start.1 = (f32[28,3,3072]{2,0,1:T(8,128)S(1)}, f32[28,3,3072]{2,0,1:T(8,128)}, u32[]{:S(2)}) copy-start(f32[28,3,3072]{2,0,1:T(8,128)} %param.10) | copy-start | bytes 3096580
Sparse Core Ops, SparseCore 0:
  10.3 92.3 all-gather.4
  104.5 37.3 all-gather.8
  152.0 97.8 reduce-scatter.5
  252.3 88.3 all-gather.6
  343.7 87.5 all-gather.10
  435.6 96.7 reduce-scatter.3
  534.8 63.2 reduce-scatter.7
where the time goes:
time: 610 us; the launch traced here: 607 us
  waiting for transfers between devices  516 us (85%)
  matrix products  48.6 us (8%)
  other arithmetic  25.6 us (4%)
  between operations  15 us (2%)
    reduce_scatter x1, waiting for transfers between devices, per_device(): lax.psum_scatter(velocity_part.astype(jnp.bfloat16), 'mp', scatter_dimens...  97.4 us
    all_gather x1, waiting for transfers between devices, per_device(): lax.all_gather(states, 'mp', axis=1, tiled=True)  92.7 us
    all_gather x1, waiting for transfers between devices, per_device(): lax.all_gather(adjoint, 'mp', axis=1, tiled=True)  88.2 us
    reduce_scatter x1, waiting for transfers between devices, per_device(): lax.psum_scatter(vector_jacobian_share.astype(jnp.bfloat16), 'mp', scatte...  80.5 us
    all_gather x1, waiting for transfers between devices, per_device(): weighted_total = lax.all_gather(weighted, 'mp', axis=1, tiled=True)  69.6 us
    reduce_scatter x1, waiting for transfers between devices, per_device(): lax.psum_scatter((jnp.einsum('vzc,vza->ca', weighted_total, activation_ou...  60.5 us
    all_gather x1, waiting for transfers between devices, per_device(): lax.all_gather(offset, 'dp', axis=0, tiled=True)  24.8 us
    dot_general x1, matrix products, per_device(): jnp.einsum('ceu,nu->cen', hidden_gradient, up_projection_weight, preferre...  20.9 us
  transfers between devices with their start and end apart: 7, of which 7 were waited for; matrix products, arithmetic and copies ran while one was open for 10% of the time, Pallas kernels for 0%

commit v1 on v0

v1 whole, which is shorter than its diff:
```python
import functools
import math

import jax
import jax.numpy as jnp
from jax import lax
from jax.experimental import pallas as pl
from jax.experimental.pallas import tpu as pltpu
from jax.sharding import PartitionSpec as P

MESH = pl.DeviceIdType.MESH
BF = jnp.bfloat16
F32 = jnp.float32
D = 3072
T = 128
HH = 768
NT = (((1,), (1,)), ((), ()))
NN = (((1,), (0,)), ((), ()))
N_MSG = 80


def gelu_both(value):
    coeff = math.sqrt(2.0 / math.pi)
    square = value * value
    tangent = jnp.tanh(coeff * value * (1.0 + 0.044715 * square))
    half = 0.5 * (1.0 + tangent)
    slope = half + 0.5 * value * (1.0 - tangent * tangent) * coeff * (1.0 + 3.0 * 0.044715 * square)
    return value * half, slope


def dot(a, b, dims):
    return lax.dot_general(a, b, dims, preferred_element_type=F32)


def loop(count, body):
    def step(i, carry):
        body(i)
        return carry

    lax.fori_loop(0, count, step, 0)


def kernel(
    mod_in, gat_in, adj_in, rows_in, up_in, down_in, off_in,
    gm_out, og_out,
    modb, gatb, upb, downb, ofs, actb, slp, ghb, sopp, sun, sai, pown,
    vA, vB, vL, vR, jA, jB, jL, jR, gcore, zA, zB, zL, zR, ysum, yr,
    ss, rs, ls,
):
    dp, mp = lax.axis_index("dp"), lax.axis_index("mp")
    c, z, yl = dp % 2, (dp // 2) % 4, dp // 8
    x, yh = mp % 4, mp // 4
    y = yh * 2 + yl

    def dev(xx, yy, zz, cc):
        return (((yy % 2) * 4 + zz) * 2 + cc, (yy // 2) * 4 + xx)

    right, left = dev((x + 1) % 4, y, z, c), dev((x + 3) % 4, y, z, c)
    z_up, z_dn = (z + 1) % 4, (z + 3) % 4
    z_op = (z + 2) % 4
    zright, zleft = dev(x, y, z_up, c), dev(x, y, z_dn, c)
    y_up, y_dn, y_op = (y + 1) % 4, (y + 3) % 4, (y + 2) % 4
    yright, yleft, yfar = dev(x, y_up, z, c), dev(x, y_dn, z, c), dev(x, y_op, z, c)
    ypair = dev(x, 3 - y, z, c)
    sib = dev(x, y, z, 1 - c)
    oh = 1 - yh

    count = [0]
    unsent = {}

    def send(src, dst, device):
        i = count[0]
        count[0] += 1
        msg = pltpu.make_async_remote_copy(
            src_ref=src, dst_ref=dst, send_sem=ss.at[i], recv_sem=rs.at[i],
            device_id=device, device_id_type=MESH,
        )
        msg.start()
        unsent[id(msg)] = msg
        return msg

    def sent(*msgs):
        for m in msgs:
            m.wait_send()
            del unsent[id(m)]

    def local(i, src, dst):
        copy = pltpu.make_async_copy(src, dst, ls.at[i])
        copy.start()
        return copy

    l_up = local(0, up_in, upb.at[yh])
    l_mod = local(1, mod_in, modb.at[0])
    l_off = local(2, off_in, ofs.at[yh, yl, z, c])
    l_gat = local(3, gat_in, gatb.at[0])
    l_down = local(4, down_in, downb.at[yh])

    barrier = pltpu.get_barrier_semaphore()
    peers = (right, left, zright, zleft, yright, yleft, yfar, sib)
    for peer in peers:
        pl.semaphore_signal(barrier, inc=1, device_id=peer, device_id_type=MESH)
    pl.semaphore_wait(barrier, len(peers))

    lo, hi = pl.ds(0, T // 2), pl.ds(T // 2, T // 2)

    def xg_start(src, buf):
        return send(src, buf.at[1], right), send(src, buf.at[2], left)

    def xg_mid(buf, first):
        first[0].wait_recv()
        a = send(buf.at[1, lo], buf.at[3, lo], right)
        first[1].wait_recv()
        b = send(buf.at[2, hi], buf.at[3, hi], left)
        return a, b

    def arrived(msgs):
        for m in msgs:
            m.wait_recv()

    def rows_of(zz, cc, size, half=None):
        if half is None:
            return pl.ds((zz * 2 + cc) * size, size)
        return pl.ds((zz * 2 + cc) * size + half * (size // 2), size // 2)

    def w_start(src, buf, size):
        r = rows_of(z, c, size)
        return send(src.at[r], buf.at[yh, r], ypair)

    def w_ring(buf, size, first):
        first.wait_recv()
        piece = buf.at[oh, rows_of(z, c, size)]
        return send(piece, piece, zright), send(piece, piece, zleft), send(piece, piece, sib)

    def w_mid(buf, size, msgs):
        msgs[0].wait_recv()
        a_ref = buf.at[oh, rows_of(z_dn, c, size, 0)]
        a = send(a_ref, a_ref, zright)
        msgs[1].wait_recv()
        b_ref = buf.at[oh, rows_of(z_up, c, size, 1)]
        b = send(b_ref, b_ref, zleft)
        p, q = buf.at[oh, rows_of(z_dn, c, size)], buf.at[oh, rows_of(z_up, c, size)]
        return a, b, send(p, p, sib), send(q, q, sib)

    def w_end(buf, size, msgs):
        msgs[0].wait_recv()
        msgs[1].wait_recv()
        p = buf.at[oh, rows_of(z_op, c, size)]
        return send(p, p, sib)

    USZ, DSZ = D // 8, HH // 8

    m1 = xg_start(mod_in, modb)
    u1 = w_start(up_in, upb, USZ)
    ob = ofs.at[yh, yl, z, c]
    o1 = (send(off_in, ob, zright), send(off_in, ob, zleft))

    def p_hidden(h, row0, rows, slot0):
        slots = rows // T

        def body(j):
            cols = pl.ds(pl.multiple_of(j * 256, 256), 256)
            mod = modb[pl.ds(slot0, slots)].reshape(rows, D)
            act, slope = gelu_both(dot(mod, upb[h, :, cols], NN))
            actb[h, pl.ds(row0, rows), cols] = act.astype(BF)
            slp[h, pl.ds(row0, rows), cols] = slope

        loop(HH // 256, body)

    def p_gh(h, row0, rows, slot0):
        slots = rows // T

        def body(j):
            off = pl.multiple_of(j * 256, 256)
            cols = pl.ds(off, 256)
            gat = gatb[pl.ds(slot0, slots)].reshape(rows, D)
            grad = dot(gat, downb[h, pl.ds(off, 256), :], NT)
            ghb[h, pl.ds(row0, rows), cols] = (grad * slp[h, pl.ds(row0, rows), cols]).astype(BF)

        loop(HH // 256, body)

    l_mod.wait()
    l_up.wait()
    p_hidden(yh, 0, T, 0)

    l_off.wait()
    o1[0].wait_recv()
    hA, hB = pl.ds(0, 96), pl.ds(96, 96)
    r1 = ofs.at[yh, yl, z_dn, c, hA]
    o2a = send(r1, r1, zright)
    o1[1].wait_recv()
    r2 = ofs.at[yh, yl, z_up, c, hB]
    o2b = send(r2, r2, zleft)
    arrived((o2a, o2b))
    bundle = ofs.at[yh, yl, :, c]
    o3 = (send(bundle, bundle, yright), send(bundle, bundle, yleft), send(bundle, bundle, sib))

    u2 = w_ring(upb, USZ, u1)

    m2 = xg_mid(modb, m1)
    l_gat.wait()
    g1 = xg_start(gat_in, gatb)
    p_hidden(yh, T, 2 * T, 1)
    u3 = w_mid(upb, USZ, u2)
    arrived(m2)
    p_hidden(yh, 3 * T, T, 3)
    u4 = w_end(upb, USZ, u3)

    def ybundle(yy, half=None):
        if half is None:
            return ofs.at[yy // 2, yy % 2, :, c]
        return ofs.at[yy // 2, yy % 2, pl.ds(2 * half, 2), c]

    o3[0].wait_recv()
    r3 = ybundle(y_dn, 0)
    o4a = send(r3, r3, yright)
    o3[1].wait_recv()
    r4 = ybundle(y_up, 1)
    o4b = send(r4, r4, yleft)
    r5, r6 = ybundle(y_dn), ybundle(y_up)
    o4c, o4d = send(r5, r5, sib), send(r6, r6, sib)
    d1 = w_start(down_in, downb, DSZ)

    arrived((u2[2], u3[2], u3[3], u4))
    p_hidden(oh, 0, 4 * T, 0)

    g2 = xg_mid(gatb, g1)
    l_down.wait()
    p_gh(yh, 0, 3 * T, 0)
    arrived((o4a, o4b))
    r7 = ybundle(y_op)
    o5 = send(r7, r7, sib)
    arrived(g2)
    p_gh(yh, 3 * T, T, 3)
    arrived((o3[2], o4c, o4d, o5))
    d2 = w_ring(downb, DSZ, d1)

    def tile_sum(src, wt, rows, j):
        acc = None
        for h in range(2):
            lhs = [src[h, r, :] for r in rows]
            lhs = lhs[0] if len(lhs) == 1 else jnp.concatenate(lhs, axis=0)
            part = dot(lhs, wt(h, j), NT)
            acc = part if acc is None else acc + part
        return acc

    def cols_of(j):
        return pl.ds(pl.multiple_of(j * 384, 384), 384)

    def wt_off(h, j):
        return ofs[h, j // 4, j % 4].reshape(384, HH)

    def wt_up(h, j):
        return upb[h, pl.ds(pl.multiple_of(j * 384, 384), 384), :]

    OWN, FAR = (pl.ds(0, T),), (pl.ds(3 * T, T),)
    UNAIDED = (pl.ds(T + 64, T),)
    AIDED = (pl.ds(T, 64), pl.ds(2 * T + 64, 64))

    def rs_far(src, wt, A, B):
        def body(j):
            sopp[:, cols_of(j)] = tile_sum(src, wt, FAR, j).astype(BF)

        loop(8, body)
        return send(sopp.at[lo], A, left), send(sopp.at[hi], B, right)

    def rs_near(src, wt, fL, fR):
        def body(j):
            sun[:, cols_of(j)] = tile_sum(src, wt, UNAIDED, j).astype(BF)

        loop(8, body)
        return send(sun.at[lo], fR.at[hi], left), send(sun.at[hi], fL.at[lo], right)

    def rs_own(src, wt):
        def body(j):
            pown[:, cols_of(j)] = tile_sum(src, wt, OWN, j)

        loop(8, body)

    def rs_aided(src, wt, A, B, first, fL, fR):
        arrived(first)

        def body(j):
            acc = tile_sum(src, wt, AIDED, j)
            came = jnp.concatenate([A[:, cols_of(j)], B[:, cols_of(j)]], axis=0)
            sai[:, cols_of(j)] = (acc + came.astype(F32)).astype(BF)

        loop(8, body)
        return send(sai.at[lo], fR.at[lo], left), send(sai.at[hi], fL.at[hi], right)

    v1 = rs_far(actb, wt_off, vA, vB)
    v2 = rs_near(actb, wt_off, vL, vR)
    d3 = w_mid(downb, DSZ, d2)
    rs_own(actb, wt_off)
    sent(*m1, *m2)
    v3 = rs_aided(actb, wt_off, vA, vB, v1, vL, vR)
    d4 = w_end(downb, DSZ, d3)
    arrived((d2[2], d3[2], d3[3], d4))
    p_gh(oh, 0, 4 * T, 0)
    arrived(v2 + v3)

    def weigh(j):
        cols = cols_of(j)
        gap = pown[:, cols] + vL[:, cols].astype(F32) + vR[:, cols].astype(F32)
        rows = rows_in[:, cols]
        res = rows[1:2] * gap + rows[0:1] * adj_in[:, cols].astype(F32)
        modb[0, :, cols] = res.astype(BF)

    loop(8, weigh)
    w1 = xg_start(modb.at[0], modb)

    sent(*v1, *v2, *v3)
    j1 = rs_far(ghb, wt_up, jA, jB)
    j2 = rs_near(ghb, wt_up, jL, jR)
    rs_own(ghb, wt_up)
    w2 = xg_mid(modb, w1)
    j3 = rs_aided(ghb, wt_up, jA, jB, j1, jL, jR)

    sent(*o1, o2a, o2b, *o3, o4a, o4b, o4c, o4d, o5)
    arrived(w2)

    def g_part(zz):
        def body(yy):
            cols = pl.ds(pl.multiple_of((yy * 4 + zz) * 384, 384), 384)
            wt = modb[:, :, cols].reshape(4 * T, 384).T
            for h in range(2):
                ofs[h, yy, zz] = dot(wt, actb[h], NN).astype(BF).reshape(2, 192, HH)

        loop(2, body)
        return send(ofs.at[:, :, zz, 1 - c], gcore.at[:, :, zz], sib)

    def g_add(zz, halves, extra=None):
        def body(yy):
            for h in halves:
                total = ofs[h, yy, zz, c].astype(F32) + gcore[h, yy, zz].astype(F32)
                if extra is not None:
                    total = total + extra[yy].astype(F32)
                ofs[h, yy, zz, c] = total.astype(BF)

        loop(2, body)

    c_op = g_part(z_op)
    c_dn = g_part(z_dn)
    arrived((c_op,))
    g_add(z_op, (0, 1))
    q1 = (
        send(ofs.at[0, :, z_op, c], zA, zleft),
        send(ofs.at[1, :, z_op, c], zB, zright),
    )
    c_up = g_part(z_up)
    arrived((c_dn, c_up))
    g_add(z_dn, (1,))
    q2a = send(ofs.at[1, :, z_dn, c], zR.at[1], zleft)
    g_add(z_up, (0,))
    q2b = send(ofs.at[0, :, z_up, c], zL.at[0], zright)
    c_own = g_part(z)
    arrived(q1)
    g_add(z_dn, (0,), zA)
    q3a = send(ofs.at[0, :, z_dn, c], zR.at[0], zleft)
    g_add(z_up, (1,), zB)
    q3b = send(ofs.at[1, :, z_up, c], zL.at[1], zright)

    arrived(j2 + j3)

    def finish(j):
        cols = cols_of(j)
        gm_out[:, cols] = pown[:, cols] + jL[:, cols].astype(F32) + jR[:, cols].astype(F32)

    loop(8, finish)

    arrived((c_own, q2a, q2b, q3a, q3b))

    def g_sum(yy):
        h, k = yy // 2, yy % 2
        return (
            ofs[h, k, z, c].astype(F32)
            + gcore[h, k, z].astype(F32)
            + zL[h, k].astype(F32)
            + zR[h, k].astype(F32)
        )

    def g_out(i, target):
        yy = (y_op, y_up, y_dn)[i]
        ysum[i] = g_sum(yy).astype(BF)
        return send(ysum.at[i], yr.at[i], target)

    e = [g_out(0, yfar), g_out(1, yright), g_out(2, yleft)]
    og_out[...] = g_sum(y)
    arrived(e)
    og_out[...] = (
        og_out[...] + yr[0].astype(F32) + yr[1].astype(F32) + yr[2].astype(F32)
    ) * (1.0 / 128.0)
    for m in list(unsent.values()):
        sent(m)


def fused(mod, gated, adj, rows, up, down, off):
    hbm = pl.BlockSpec(memory_space=pl.ANY)
    vmem = pl.BlockSpec(memory_space=pltpu.VMEM)
    V = pltpu.VMEM
    flops = 5 * 2 * 1024 * D * HH
    return pl.pallas_call(
        kernel,
        out_shape=(
            jax.ShapeDtypeStruct((T, D), F32),
            jax.ShapeDtypeStruct((192, HH), F32),
        ),
        in_specs=[hbm, hbm, vmem, vmem, hbm, hbm, hbm],
        out_specs=(vmem, vmem),
        scratch_shapes=[
            V((4, T, D), BF), V((4, T, D), BF),
            V((2, D, HH), BF), V((2, HH, D), BF),
            V((2, 2, 4, 2, 192, HH), BF),
            V((2, 4 * T, HH), BF), V((2, 4 * T, HH), F32), V((2, 4 * T, HH), BF),
            V((T, D), BF), V((T, D), BF), V((T, D), BF), V((T, D), F32),
            V((64, D), BF), V((64, D), BF), V((T, D), BF), V((T, D), BF),
            V((64, D), BF), V((64, D), BF), V((T, D), BF), V((T, D), BF),
            V((2, 2, 4, 192, HH), BF),
            V((2, 192, HH), BF), V((2, 192, HH), BF),
            V((2, 2, 192, HH), BF), V((2, 2, 192, HH), BF),
            V((3, 192, HH), BF), V((3, 192, HH), BF),
            pltpu.SemaphoreType.DMA((N_MSG,)),
            pltpu.SemaphoreType.DMA((N_MSG,)),
            pltpu.SemaphoreType.DMA((5,)),
        ],
        compiler_params=pltpu.CompilerParams(
            collective_id=0, has_side_effects=True, vmem_limit_bytes=64 << 20
        ),
        cost_estimate=pl.CostEstimate(flops=flops, bytes_accessed=40 << 20, transcendentals=1 << 20),
        name="fused_step",
    )(mod, gated, adj, rows, up, down, off)


def per_device(states, adjoint, step_index, modulation, up, down, offset):
    step_count = modulation.shape[0]
    index = step_index[0]
    mods = lax.dynamic_index_in_dim(modulation, index, 0, keepdims=False)
    shift, scale, gate = mods[0:1], mods[1:2], mods[2:3]
    timing = (index.astype(F32) + 1.0) / (step_count + 1.0)
    variance = 2.0 * (1.0 - timing) / timing
    inputs = states[0].astype(F32)
    mean = jnp.mean(inputs, axis=-1, keepdims=True)
    var = jnp.mean((inputs - mean) ** 2, axis=-1, keepdims=True)
    rstd = lax.rsqrt(var + 1e-06)
    normed = (inputs - mean) * rstd
    modulated = (normed * (1.0 + scale) + shift).astype(BF)
    adj = adjoint[0]
    gated = (adj.astype(F32) * gate).astype(BF)
    rows = jnp.concatenate([gate, 2.0 / variance * gate * gate] + [gate] * 6, axis=0)
    grad_mod, offset_grad = fused(modulated, gated, adj, rows, up, down, offset)
    scaled = grad_mod * (1.0 + scale)
    adjoint_rate = rstd * (
        scaled
        - jnp.mean(scaled, axis=-1, keepdims=True)
        - normed * jnp.mean(scaled * normed, axis=-1, keepdims=True)
    )
    return adjoint_rate[None], offset_grad


def solution(mesh):
    in_specs = (
        P("dp", "mp", None),
        P("dp", "mp", None),
        P("dp"),
        P(),
        P(None, "mp"),
        P("mp", None),
        P("dp", "mp"),
    )
    out_specs = (P("dp", "mp", None), P("dp", "mp"))
    return jax.shard_map(
        per_device, mesh=mesh, in_specs=in_specs, out_specs=out_specs, check_vma=False
    )
```

time: 610 us -> 226 us (0.37)
  waiting for transfers between devices: 516 us -> 0 us
  Pallas kernels: 0 us -> 212 us
  matrix products: 48.6 us -> 0 us
  other arithmetic: 25.6 us -> 10.3 us
  between operations: 15 us -> 1.57 us
    all_gather x4 -> x0, waiting for transfers between devices: 275 us -> none  [the longest x1 92.7 us: per_device(): lax.all_gather(states, 'mp', axis=1, tiled=True)]
    reduce_scatter x3 -> x0, waiting for transfers between devices: 238 us -> none  [the longest x1 97.4 us: per_device(): lax.psum_scatter(velocity_part.astype(jnp.bfloat16), 'mp', scatter_dimens...]
    pallas_call x0 -> x1, Pallas kernels: none -> 212 us  [fused(): pl.pallas_call(kernel, out_shape=(jax.ShapeDtypeStruct((T, D), F32), jax....]
    dot_general x5 -> x0, matrix products: 48.6 us -> none  [the longest x1 20.9 us: per_device(): jnp.einsum('ceu,nu->cen', hidden_gradient, up_projection_weight, preferre...]
    mul x2 -> x1, other arithmetic: 13.8 us -> 0.92 us  [per_device(): 2.0 / variance * gate * gate]
  transfers between devices with their start and end apart: 7 -> 0, of which waited for: 7 -> 0; matrix products, arithmetic and copies ran while one was open for 10% -> 0% of each run, Pallas kernels for 0% -> 0%
where the time goes in v1:
time: 226 us
  Pallas kernels  212 us (94%)
  other arithmetic  10.3 us (5%)
    pallas_call x1, Pallas kernels, fused(): pl.pallas_call(kernel, out_shape=(jax.ShapeDtypeStruct((T, D), F32), jax....  212 us

profile of v1, /device:TPU:1, one launch (start us, length us, event | category | flops | bytes accessed | tf_op | source)
XLA Modules:
  0.0 225.8 jit_solution(12113021309206595776)
XLA Ops:
  0.6 0.0 copy-start
  0.6 0.0 copy-start.3
  1.5 1.3 convert_reduce_fusion
  2.8 0.0 copy-start.7
  2.8 1.5 fusion.12
  4.3 0.0 copy-start.9
  4.3 0.9 multiply_multiply_fusion
  5.2 1.0 dynamic-slice_add_fusion
  6.2 0.0 copy-start.5
  6.2 0.8 concatenate.3.rows_in
  7.0 0.0 copy-done
  7.0 0.0 copy-done.3
  7.0 1.6 fusion.7
  8.6 0.0 copy-done.9
  8.6 0.0 copy-done.5
  8.6 0.0 copy-done.7
  8.6 212.3 %fused_step.1 = (f32[128,3072]{1,0:T(8,128)}, f32[192,768]{1,0:T(8,128)}) custom-call(bf16[128,3072]{1,0:T(8,128)(2,1)} %get-tuple-element.12.mod_in, bf16[128,3072]{1,0:T(8,128)(2,1)} %get-tuple-element.13.gat_in, bf16[128,3072]{1,0:T(8,128)(2,1)} %bitcast.50, f32[8,3072]{1,0:T(8,128)} %concatenate.3.rows_in, bf16[3072,768]{1,0:T(8,128)(2,1)} %up_in.1, ...), custom_call_target="tpu_custom_call" | custom-call | flops 24159191040 | bytes 41943040 | tf_op jit(solution)/shard_map/fused_step/pallas_call | solution.py:401
  220.9 0.0 copy-start.1
  220.9 0.0 copy-start.2
  220.9 0.0 copy-start.6
  220.9 0.0 copy-start.8
  220.9 0.0 copy-start.10
  220.9 2.3 multiply_reduce_fusion
  223.2 0.0 copy-done.1
  223.2 0.1 copy-done.2
  223.3 0.0 copy-done.6
  223.3 0.0 copy-done.8
  223.3 0.0 copy-done.10
  223.3 0.0 copy-start.4
  223.3 1.7 fusion.11
  225.0 0.0 copy-done.4
  225.0 0.8 copy.11
  (4 shorter events, 0.0 us)
Async XLA Ops:
  0.6 6.4 %copy-start = (bf16[1,128,3072]{2,1,0:T(8,128)(2,1)S(1)}, bf16[1,128,3072]{2,1,0:T(8,128)(2,1)}, u32[]{:S(2)}) copy-start(bf16[1,128,3072]{2,1,0:T(8,128)(2,1)} %param.7) | copy-start | bytes 2359300
  0.6 6.4 %copy-start.3 = (bf16[1,128,3072]{2,1,0:T(8,128)(2,1)S(1)}, bf16[1,128,3072]{2,1,0:T(8,128)(2,1)}, u32[]{:S(2)}) copy-start(bf16[1,128,3072]{2,1,0:T(8,128)(2,1)} %param.8) | copy-start | bytes 2359300
  2.8 5.8 %copy-start.7 = (f32[128]{0:T(128)}, f32[128]{0:T(128)S(1)}, u32[]{:S(2)}) copy-start(f32[128]{0:T(128)S(1)} %broadcast_multiply_fusion.2) | copy-start | bytes 1540
  4.3 4.3 %copy-start.9 = (f32[128]{0:T(128)}, f32[128]{0:T(128)S(1)}, u32[]{:S(2)}) copy-start(f32[128]{0:T(128)S(1)} %add_rsqrt_fusion) | copy-start | bytes 1540
  6.2 2.4 %copy-start.5 = (f32[1,1,3072]{2,0,1:T(1,128)}, f32[1,1,3072]{2,0,1:T(1,128)S(1)}, u32[]{:S(2)}) copy-start(f32[1,1,3072]{2,0,1:T(1,128)S(1)} %get-tuple-element.10) | copy-start | bytes 36868
  220.9 2.3 %copy-start.1 = (bf16[1,128,3072]{2,1,0:T(8,128)(2,1)S(1)}, bf16[1,128,3072]{2,1,0:T(8,128)(2,1)}, u32[]{:S(2)}) copy-start(bf16[1,128,3072]{2,1,0:T(8,128)(2,1)} %param.7) | copy-start | bytes 2359300
  220.9 2.4 %copy-start.2 = (f32[128,3072]{1,0:T(8,128)S(1)}, f32[128,3072]{1,0:T(8,128)}, u32[]{:S(2)}) copy-start(f32[128,3072]{1,0:T(8,128)} %get-tuple-element.4) | copy-start | bytes 4718596
  220.9 2.4 %copy-start.6 = (f32[1,1,3072]{2,0,1:T(1,128)S(1)}, f32[1,1,3072]{2,0,1:T(1,128)}, u32[]{:S(2)}) copy-start(f32[1,1,3072]{2,0,1:T(1,128)} %copy-done.5) | copy-start | bytes 36868
  220.9 2.4 %copy-start.8 = (f32[128]{0:T(128)S(1)}, f32[128]{0:T(128)}, u32[]{:S(2)}) copy-start(f32[128]{0:T(128)} %copy-done.7) | copy-start | bytes 1540
  220.9 2.4 %copy-start.10 = (f32[128]{0:T(128)S(1)}, f32[128]{0:T(128)}, u32[]{:S(2)}) copy-start(f32[128]{0:T(128)} %copy-done.9) | copy-start | bytes 1540
  223.3 1.7 copy-start.4

commit v2 on v0

v2 whole, which is shorter than its diff:
```python
import functools
import math

import jax
import jax.numpy as jnp
from jax import lax
from jax.experimental import pallas as pl
from jax.experimental.pallas import tpu as pltpu
from jax.sharding import PartitionSpec as P

MESH = pl.DeviceIdType.MESH
BF = jnp.bfloat16
F32 = jnp.float32
D = 3072
T = 128
HH = 768
NT = (((1,), (1,)), ((), ()))
NN = (((1,), (0,)), ((), ()))
N_MSG = 144


def gelu_both(value):
    coeff = math.sqrt(2.0 / math.pi)
    square = value * value
    tangent = jnp.tanh(coeff * value * (1.0 + 0.044715 * square))
    half = 0.5 * (1.0 + tangent)
    slope = half + 0.5 * value * (1.0 - tangent * tangent) * coeff * (1.0 + 3.0 * 0.044715 * square)
    return value * half, slope


def dot(a, b, dims):
    return lax.dot_general(a, b, dims, preferred_element_type=F32)


def loop(count, body):
    def step(i, carry):
        body(i)
        return carry

    lax.fori_loop(0, count, step, 0)


def kernel(
    st_in, adj_in, rows_in, up_in, down_in, off_in,
    rate_out, og_out,
    modb, gatb, upb, downb, ofs, actb, slp, ghb, sact, swgt, sopp, sun, sai, aid,
    vA, vB, vL, vR, jA, jB, jL, jR, zA, zB, zL, zR, yA, yB, yL, yR, ysum, yr, zsum, zr,
    ss, rs, ls,
):
    dp, mp = lax.axis_index("dp"), lax.axis_index("mp")
    c, z, yl = dp % 2, (dp // 2) % 4, dp // 8
    x, yh = mp % 4, mp // 4
    y = yh * 2 + yl

    def dev(xx, yy, zz, cc):
        return (((yy % 2) * 4 + zz) * 2 + cc, (yy // 2) * 4 + xx)

    right, left = dev((x + 1) % 4, y, z, c), dev((x + 3) % 4, y, z, c)
    z_up, z_dn, z_op = (z + 1) % 4, (z + 3) % 4, (z + 2) % 4
    y_up, y_dn, y_op = (y + 1) % 4, (y + 3) % 4, (y + 2) % 4
    zright, zleft, zfar = dev(x, y, z_up, c), dev(x, y, z_dn, c), dev(x, y, z_op, c)
    yright, yleft, yfar = dev(x, y_up, z, c), dev(x, y_dn, z, c), dev(x, y_op, z, c)
    ypair = dev(x, 3 - y, z, c)
    sib = dev(x, y, z, 1 - c)
    oh = 1 - yh

    count = [0]
    unsent = {}

    def send(src, dst, device):
        i = count[0]
        count[0] += 1
        msg = pltpu.make_async_remote_copy(
            src_ref=src, dst_ref=dst, send_sem=ss.at[i], recv_sem=rs.at[i],
            device_id=device, device_id_type=MESH,
        )
        msg.start()
        unsent[id(msg)] = msg
        return msg

    def sent(msgs):
        for m in msgs:
            m.wait_send()
            del unsent[id(m)]

    def arrived(msgs):
        for m in msgs:
            m.wait_recv()

    def local(i, src, dst):
        copy = pltpu.make_async_copy(src, dst, ls.at[i])
        copy.start()
        return copy

    l_up = local(0, up_in, upb.at[yh])
    l_off = local(1, off_in, ofs.at[yh, c, yl, z])
    l_down = local(2, down_in, downb.at[yh])

    barrier = pltpu.get_barrier_semaphore()
    peers = (right, left, zright, zleft, zfar, yright, yleft, yfar, sib)
    for peer in peers:
        pl.semaphore_signal(barrier, inc=1, device_id=peer, device_id_type=MESH)
    pl.semaphore_wait(barrier, len(peers))

    lo, hi = pl.ds(0, T // 2), pl.ds(T // 2, T // 2)
    E0, E1 = pl.ds(0, 384), pl.ds(384, 384)

    def ring_start(src, own, nxt, prv):
        return [send(src, own, nxt), send(src, own, prv)]

    def ring_mid(first, from_prv, from_nxt, nxt, prv):
        first[0].wait_recv()
        a = send(from_prv, from_prv, nxt)
        first[1].wait_recv()
        b = send(from_nxt, from_nxt, prv)
        return [a, b]

    def xg_start(buf, cols):
        src = buf.at[0, :, cols]
        return [send(src, buf.at[1, :, cols], right), send(src, buf.at[2, :, cols], left)]

    def xg_mid(buf, cols, first):
        first[0].wait_recv()
        a = send(buf.at[1, lo, cols], buf.at[3, lo, cols], right)
        first[1].wait_recv()
        b = send(buf.at[2, hi, cols], buf.at[3, hi, cols], left)
        return [a, b]

    def piece(buf, zz, size, half=None):
        first = (zz * 2 + c) * size
        if half is None:
            return buf.at[oh, pl.ds(first, size)]
        return buf.at[oh, pl.ds(first + half * (size // 2), size // 2)]

    def w_start(src, buf, size):
        r = pl.ds((z * 2 + c) * size, size)
        return send(src.at[r], buf.at[yh, r], ypair)

    def w_ring(buf, size, first):
        first.wait_recv()
        p = piece(buf, z, size)
        return ring_start(p, p, zright, zleft) + [send(p, p, sib)]

    def w_mid(buf, size, msgs):
        out = ring_mid(msgs, piece(buf, z_dn, size, 0), piece(buf, z_up, size, 1), zright, zleft)
        p, q = piece(buf, z_dn, size), piece(buf, z_up, size)
        return out + [send(p, p, sib), send(q, q, sib)]

    def w_end(buf, size, msgs):
        arrived(msgs[:2])
        p = piece(buf, z_op, size)
        return [send(p, p, sib)]

    USZ, DSZ = D // 8, HH // 8
    ALL = pl.ds(0, D)

    def oblock(yy, zz, cols, half=None):
        rows = pl.ds(0, 192) if half is None else pl.ds(96 * half, 96)
        return ofs.at[yy // 2, c, yy % 2, zz, rows, cols]

    def ybundle(yy, half=None):
        zs = pl.ds(0, 4) if half is None else pl.ds(2 * half, 2)
        return ofs.at[yy // 2, c, yy % 2, zs, :, E0]

    def zbundle(zz, half=None):
        hs = pl.ds(0, 2) if half is None else pl.ds(half, 1)
        return ofs.at[hs, c, :, zz, :, E1]

    u1 = w_start(up_in, upb, USZ)
    oA = ring_start(off_in.at[:, E0], oblock(y, z, E0), zright, zleft)
    oB = ring_start(off_in.at[:, E1], oblock(y, z, E1), yright, yleft)

    def norm_of(rows):
        inputs = st_in[rows, :].astype(F32)
        mean = jnp.mean(inputs, axis=-1, keepdims=True)
        cent = inputs - mean
        var = jnp.mean(cent * cent, axis=-1, keepdims=True)
        rstd = lax.rsqrt(var + 1e-06)
        return cent * rstd, rstd

    def prepare(i):
        rows = pl.ds(pl.multiple_of(i * 16, 16), 16)
        normed, _ = norm_of(rows)
        modb[0, rows, :] = (normed * rows_in[3:4, :] + rows_in[2:3, :]).astype(BF)
        gatb[0, rows, :] = (adj_in[rows, :].astype(F32) * rows_in[0:1, :]).astype(BF)

    loop(T // 16, prepare)
    m1 = xg_start(modb, ALL)

    def p_hidden(h, row0, rows, slot0):
        def body(j):
            cols = pl.ds(pl.multiple_of(j * 256, 256), 256)
            mod = modb[pl.ds(slot0, rows // T)].reshape(rows, D)
            act, slope = gelu_both(dot(mod, upb[h, :, cols], NN))
            actb[h, pl.ds(row0, rows), cols] = act.astype(BF)
            slp[h, pl.ds(row0, rows), cols] = slope

        loop(HH // 256, body)

    def p_gh(h, row0, rows, slot0):
        def body(j):
            off = pl.multiple_of(j * 256, 256)
            cols = pl.ds(off, 256)
            gat = gatb[pl.ds(slot0, rows // T)].reshape(rows, D)
            grad = dot(gat, downb[h, pl.ds(off, 256), :], NT)
            ghb[h, pl.ds(row0, rows), cols] = (grad * slp[h, pl.ds(row0, rows), cols]).astype(BF)

        loop(HH // 256, body)

    l_up.wait()
    p_hidden(yh, 0, T, 0)

    l_off.wait()
    oA2 = ring_mid(oA, oblock(y, z_dn, E0, 0), oblock(y, z_up, E0, 1), zright, zleft)
    oB2 = ring_mid(oB, oblock(y_dn, z, E1, 0), oblock(y_up, z, E1, 1), yright, yleft)
    arrived(oA2)
    yb = ybundle(y)
    oC = ring_start(yb, yb, yright, yleft) + [send(yb, yb, sib)]
    arrived(oB2)
    u2 = w_ring(upb, USZ, u1)
    zb = zbundle(z)
    oD = ring_start(zb, zb, zright, zleft) + [send(zb, zb, sib)]

    m2 = xg_mid(modb, ALL, m1)
    g1 = xg_start(gatb, ALL)
    p_hidden(yh, T, 2 * T, 1)
    u3 = w_mid(upb, USZ, u2)
    arrived(m2)
    p_hidden(yh, 3 * T, T, 3)
    a1 = send(actb.at[yh], sact.at[yh], sib)

    oC2 = ring_mid(oC, ybundle(y_dn, 0), ybundle(y_up, 1), yright, yleft)
    d1 = w_start(down_in, downb, DSZ)
    yd, yu = ybundle(y_dn), ybundle(y_up)
    oC3 = [send(yd, yd, sib), send(yu, yu, sib)]
    oD2 = ring_mid(oD, zbundle(z_dn, 0), zbundle(z_up, 1), zright, zleft)
    zd, zu = zbundle(z_dn), zbundle(z_up)
    oD3 = [send(zd, zd, sib), send(zu, zu, sib)]
    u4 = w_end(upb, USZ, u3)

    g2 = xg_mid(gatb, ALL, g1)
    arrived([u2[2], u3[2], u3[3]] + u4)
    p_hidden(oh, 0, 4 * T, 0)
    a2 = send(actb.at[oh], sact.at[oh], sib)
    arrived(oC2)
    yo = ybundle(y_op)
    oC4 = [send(yo, yo, sib)]
    arrived(oD2)
    zo = zbundle(z_op)
    oD4 = [send(zo, zo, sib)]
    d2 = w_ring(downb, DSZ, d1)
    arrived([oC[2], oD[2]] + oC3 + oC4 + oD3 + oD4)

    def sum_chunk(src, wt, q, k):
        cols = pl.ds(q * 768, 768)
        acc = dot(src[0], wt[0], NT) + dot(src[1], wt[1], NT)
        rate_out[:, cols] = acc[0:T]
        sopp[:, cols] = acc[3 * T :].astype(BF)
        sun[:, cols] = acc[T + 64 : 2 * T + 64].astype(BF)
        aid[k, 0:64, :] = acc[T : T + 64]
        aid[k, 64:T, :] = acc[2 * T + 64 : 3 * T]

    def send_far(cols, A, B):
        return [
            send(sopp.at[lo, cols], A.at[:, cols], left),
            send(sopp.at[hi, cols], B.at[:, cols], right),
        ]

    def send_near(cols, fL, fR):
        return [
            send(sun.at[lo, cols], fR.at[hi, cols], left),
            send(sun.at[hi, cols], fL.at[lo, cols], right),
        ]

    def add_aided(q, k, A, B):
        cols = pl.ds(q * 768, 768)
        sai[lo, cols] = (aid[k, 0:64, :] + A[:, cols].astype(F32)).astype(BF)
        sai[hi, cols] = (aid[k, 64:T, :] + B[:, cols].astype(F32)).astype(BF)

    def send_aided(cols, fL, fR):
        return [
            send(sai.at[lo, cols], fR.at[lo, cols], left),
            send(sai.at[hi, cols], fL.at[hi, cols], right),
        ]

    order = ((0, 0), (1, 0), (0, 1), (1, 1))

    def chunk_of(i):
        return order[i][0] * 2 + order[i][1]

    def ccols(i):
        return pl.ds(chunk_of(i) * 768, 768)

    def gap_calc(i):
        cc, ll = order[i]
        wt = [ofs[h, cc, ll].reshape(768, HH) for h in range(2)]
        sum_chunk((actb[0], actb[1]), wt, chunk_of(i), i % 2)
        return send_far(ccols(i), vA, vB), send_near(ccols(i), vL, vR)

    def gap_aided(i, far):
        arrived(far)
        add_aided(chunk_of(i), i % 2, vA, vB)
        return send_aided(ccols(i), vL, vR)

    def pick(value, i):
        cc, ll = order[i]
        parts = [value[:, 384 * k + 192 * cc : 384 * k + 192 * cc + 192] for k in range(4)]
        return jnp.concatenate(parts, axis=1)

    def weigh(i, near, aided):
        arrived(near + aided)
        ll = order[i][1]
        block = pl.ds(1536 * ll, 1536)
        rows = pick(rows_in[:, block], i)

        def body(t):
            r = pl.ds(pl.multiple_of(t * 32, 32), 32)
            adj = pick(adj_in[r, block].astype(F32), i)
            cols = ccols(i)
            gap = rate_out[r, cols] + vL[r, cols].astype(F32) + vR[r, cols].astype(F32)
            modb[0, r, cols] = (rows[1:2] * gap + rows[0:1] * adj).astype(BF)

        loop(T // 32, body)
        return xg_start(modb, ccols(i))

    sent(m1 + m2)
    f0, n0 = gap_calc(0)
    l_down.wait()
    p_gh(yh, 0, T, 0)
    f1, n1 = gap_calc(1)
    b0 = gap_aided(0, f0)
    p_gh(yh, T, 2 * T, 1)
    arrived(g2)
    p_gh(yh, 3 * T, T, 3)
    b1 = gap_aided(1, f1)
    f2, n2 = gap_calc(2)
    w1 = [weigh(0, n0, b0)]
    f3, n3 = gap_calc(3)
    b2 = gap_aided(2, f2)
    w1.append(weigh(1, n1, b1))
    d3 = w_mid(downb, DSZ, d2)
    b3 = gap_aided(3, f3)
    w2 = [xg_mid(modb, ccols(0), w1[0])]
    w1.append(weigh(2, n2, b2))
    w2.append(xg_mid(modb, ccols(1), w1[1]))
    w1.append(weigh(3, n3, b3))
    d4 = w_end(downb, DSZ, d3)
    arrived([d2[2], d3[2], d3[3]] + d4)
    p_gh(oh, 0, 4 * T, 0)
    w2.append(xg_mid(modb, ccols(2), w1[2]))
    sent(f0 + f1 + f2 + f3 + n0 + n1 + n2 + n3 + b0 + b1 + b2 + b3)

    def adj_calc(q):
        wt = [upb[h, q * 768 : q * 768 + 768, :] for h in range(2)]
        sum_chunk((ghb[0], ghb[1]), wt, q, q)

    def swg(ll, half):
        mine = half * 1536 + ll * 768
        return pl.ds(pl.multiple_of(mine, 768), 768)

    def to_sib(ll):
        cols = swg(ll, 1 - c)
        return send(modb.at[:, :, cols], swgt.at[ll], sib)

    adj_calc(0)
    adj_calc(1)
    w2.append(xg_mid(modb, ccols(3), w1[3]))
    arrived(w2[0] + w2[1])
    s0 = to_sib(0)
    adj_calc(2)
    adj_calc(3)
    jf = [send_far(pl.ds(0, 1536), jA, jB), send_far(pl.ds(1536, 1536), jA, jB)]
    jn = [send_near(pl.ds(0, 1536), jL, jR), send_near(pl.ds(1536, 1536), jL, jR)]
    arrived(w2[2] + w2[3])
    s1 = to_sib(1)

    sent(oA + oA2 + oB + oB2 + oC + oC2 + oC3 + oC4 + oD + oD2 + oD3 + oD4)
    arrived([a1, a2, s0, s1])

    def g_tile(h, ll, zp):
        mine = pl.multiple_of(c * 1536 + ll * 768 + zp * 384, 384)
        theirs = pl.multiple_of(zp * 384, 384)
        own = modb[:, :, pl.ds(mine, 384)].reshape(4 * T, 384).T
        other = swgt[ll, :, :, pl.ds(theirs, 384)].reshape(4 * T, 384).T
        acc = dot(own, actb[h], NN) + dot(other, sact[h], NN)
        ofs[h, c, ll, pl.ds(2 * zp, 2)] = acc.astype(BF).reshape(2, 192, HH)

    zpA, zpB = z_op // 2, z // 2

    def gy(yy, zs):
        return ofs.at[yy // 2, c, yy % 2, zs, :, E1]

    def gz(h, zz):
        return ofs.at[h, c, :, zz, :, E0]

    Z01, Z23 = pl.ds(0, 2), pl.ds(2, 2)
    g_tile(oh, yl, zpA)
    g_tile(oh, yl, zpB)
    ey1 = [send(gy(y_op, Z01), yA, yleft), send(gy(y_op, Z23), yB, yright)]
    g_tile(oh, 1 - yl, zpA)
    g_tile(yh, yl, zpA)
    g_tile(yh, 1 - yl, zpA)
    ez1 = [send(gz(0, z_op), zA, zleft), send(gz(1, z_op), zB, zright)]
    g_tile(oh, 1 - yl, zpB)
    g_tile(yh, 1 - yl, zpB)
    ey2 = [send(gy(y_dn, Z23), yR.at[Z23], yleft), send(gy(y_up, Z01), yL.at[Z01], yright)]
    g_tile(yh, yl, zpB)
    ez2 = [send(gz(1, z_dn), zR.at[1], zleft), send(gz(0, z_up), zL.at[0], zright)]

    def add_y(yy, z0, extra):
        def body(k):
            ref = ofs.at[yy // 2, c, yy % 2, z0 + k, :, E1]
            ref[...] = (ref[...].astype(F32) + extra[k].astype(F32)).astype(BF)

        loop(2, body)

    def add_z(h, zz, extra):
        def body(k):
            ref = ofs.at[h, c, k, zz, :, E0]
            ref[...] = (ref[...].astype(F32) + extra[k].astype(F32)).astype(BF)

        loop(2, body)

    arrived(ey1)
    add_y(y_dn, 0, yA)
    ey3 = [send(gy(y_dn, Z01), yR.at[Z01], yleft)]
    add_y(y_up, 2, yB)
    ey3.append(send(gy(y_up, Z23), yL.at[Z23], yright))
    arrived(ez1)
    add_z(0, z_dn, zA)
    ez3 = [send(gz(0, z_dn), zR.at[0], zleft)]
    add_z(1, z_up, zB)
    ez3.append(send(gz(1, z_up), zL.at[1], zright))

    jb = []
    for half in range(2):
        arrived(jf[half])
        for q in (2 * half, 2 * half + 1):
            add_aided(q, q, jA, jB)
        jb.append(send_aided(pl.ds(1536 * half, 1536), jL, jR))

    arrived(ey2 + ey3)

    def y_total(zz):
        return ofs[yh, c, yl, zz, :, E1].astype(F32) + yL[zz].astype(F32) + yR[zz].astype(F32)

    ez4 = []
    for k, (zz, target) in enumerate(((z_op, zfar), (z_up, zright), (z_dn, zleft))):
        zsum[k] = y_total(zz).astype(BF)
        ez4.append(send(zsum.at[k], zr.at[k], target))
    arrived(ez2 + ez3)

    def z_total(yy):
        h, k = yy // 2, yy % 2
        return ofs[h, c, k, z, :, E0].astype(F32) + zL[h, k].astype(F32) + zR[h, k].astype(F32)

    ey4 = []
    for k, (yy, target) in enumerate(((y_op, yfar), (y_up, yright), (y_dn, yleft))):
        ysum[k] = z_total(yy).astype(BF)
        ey4.append(send(ysum.at[k], yr.at[k], target))

    for half in range(2):
        arrived(jn[half] + jb[half])

    def finish(i):
        rows = pl.ds(pl.multiple_of(i * 16, 16), 16)
        normed, rstd = norm_of(rows)
        total = rate_out[rows, :] + jL[rows, :].astype(F32) + jR[rows, :].astype(F32)
        scaled = total * rows_in[3:4, :]
        mean = jnp.mean(scaled, axis=-1, keepdims=True)
        cross = jnp.mean(scaled * normed, axis=-1, keepdims=True)
        rate_out[rows, :] = rstd * (scaled - mean - normed * cross)

    loop(T // 16, finish)

    og_out[:, E1] = y_total(z)
    og_out[:, E0] = z_total(y)
    arrived(ez4)
    og_out[:, E1] = (
        og_out[:, E1] + zr[0].astype(F32) + zr[1].astype(F32) + zr[2].astype(F32)
    ) * (1.0 / 128.0)
    arrived(ey4)
    og_out[:, E0] = (
        og_out[:, E0] + yr[0].astype(F32) + yr[1].astype(F32) + yr[2].astype(F32)
    ) * (1.0 / 128.0)
    for m in list(unsent.values()):
        m.wait_send()


def fused(states, adj, rows, up, down, off):
    hbm = pl.BlockSpec(memory_space=pl.ANY)
    vmem = pl.BlockSpec(memory_space=pltpu.VMEM)
    V = pltpu.VMEM
    flops = 5 * 2 * 1024 * D * HH
    return pl.pallas_call(
        kernel,
        out_shape=(
            jax.ShapeDtypeStruct((T, D), F32),
            jax.ShapeDtypeStruct((192, HH), F32),
        ),
        in_specs=[vmem, vmem, vmem, hbm, hbm, hbm],
        out_specs=(vmem, vmem),
        scratch_shapes=[
            V((4, T, D), BF), V((4, T, D), BF),
            V((2, D, HH), BF), V((2, HH, D), BF),
            V((2, 2, 2, 4, 192, HH), BF),
            V((2, 4 * T, HH), BF), V((2, 4 * T, HH), F32), V((2, 4 * T, HH), BF),
            V((2, 4 * T, HH), BF), V((2, 4, T, HH), BF),
            V((T, D), BF), V((T, D), BF), V((T, D), BF),
            V((4, T, HH), F32),
            V((64, D), BF), V((64, D), BF), V((T, D), BF), V((T, D), BF),
            V((64, D), BF), V((64, D), BF), V((T, D), BF), V((T, D), BF),
            V((2, 192, 384), BF), V((2, 192, 384), BF),
            V((2, 2, 192, 384), BF), V((2, 2, 192, 384), BF),
            V((2, 192, 384), BF), V((2, 192, 384), BF),
            V((4, 192, 384), BF), V((4, 192, 384), BF),
            V((3, 192, 384), BF), V((3, 192, 384), BF),
            V((3, 192, 384), BF), V((3, 192, 384), BF),
            pltpu.SemaphoreType.DMA((N_MSG,)),
            pltpu.SemaphoreType.DMA((N_MSG,)),
            pltpu.SemaphoreType.DMA((3,)),
        ],
        compiler_params=pltpu.CompilerParams(
            collective_id=0, has_side_effects=True, vmem_limit_bytes=64 << 20
        ),
        cost_estimate=pl.CostEstimate(flops=flops, bytes_accessed=40 << 20, transcendentals=1 << 20),
        name="fused_step",
    )(states, adj, rows, up, down, off)


def per_device(states, adjoint, step_index, modulation, up, down, offset):
    step_count = modulation.shape[0]
    index = step_index[0]
    mods = lax.dynamic_index_in_dim(modulation, index, 0, keepdims=False)
    shift, scale, gate = mods[0:1], mods[1:2], mods[2:3]
    timing = (index.astype(F32) + 1.0) / (step_count + 1.0)
    variance = 2.0 * (1.0 - timing) / timing
    rows = jnp.concatenate(
        [gate, 2.0 / variance * gate * gate, shift, 1.0 + scale] + [gate] * 4, axis=0
    )
    rate, offset_grad = fused(states[0], adjoint[0], rows, up, down, offset)
    return rate[None], offset_grad


def solution(mesh):
    in_specs = (
        P("dp", "mp", None),
        P("dp", "mp", None),
        P("dp"),
        P(),
        P(None, "mp"),
        P("mp", None),
        P("dp", "mp"),
    )
    out_specs = (P("dp", "mp", None), P("dp", "mp"))
    return jax.shard_map(
        per_device, mesh=mesh, in_specs=in_specs, out_specs=out_specs, check_vma=False
    )
```

time: 610 us -> 177 us (0.29)
  waiting for transfers between devices: 516 us -> 0 us
  Pallas kernels: 0 us -> 169 us
  matrix products: 48.6 us -> 0 us
  other arithmetic: 25.6 us -> 1.89 us
  between operations: 15 us -> 1.35 us
    all_gather x4 -> x0, waiting for transfers between devices: 275 us -> none  [the longest x1 92.7 us: per_device(): lax.all_gather(states, 'mp', axis=1, tiled=True)]
    reduce_scatter x3 -> x0, waiting for transfers between devices: 238 us -> none  [the longest x1 97.4 us: per_device(): lax.psum_scatter(velocity_part.astype(jnp.bfloat16), 'mp', scatter_dimens...]
    pallas_call x0 -> x1, Pallas kernels: none -> 169 us  [fused(): pl.pallas_call(kernel, out_shape=(jax.ShapeDtypeStruct((T, D), F32), jax....]
    dot_general x5 -> x0, matrix products: 48.6 us -> none  [the longest x1 20.9 us: per_device(): jnp.einsum('ceu,nu->cen', hidden_gradient, up_projection_weight, preferre...]
    mul x2 -> x1, other arithmetic: 13.8 us -> 0.92 us  [per_device(): 2.0 / variance * gate * gate]
    reduce_sum x3 -> x0, other arithmetic: 7.58 us -> none  [the longest x1 3.82 us: per_device(): mean = jnp.mean(inputs, axis=-1, keepdims=True)]
  transfers between devices with their start and end apart: 7 -> 0, of which waited for: 7 -> 0; matrix products, arithmetic and copies ran while one was open for 10% -> 0% of each run, Pallas kernels for 0% -> 0%
where the time goes in v2:
time: 177 us
  Pallas kernels  169 us (95%)
  local copies, waits for them, and re-layouts  4.37 us (2%)
  other arithmetic  1.89 us (1%)
    pallas_call x1, Pallas kernels, fused(): pl.pallas_call(kernel, out_shape=(jax.ShapeDtypeStruct((T, D), F32), jax....  169 us
    unnamed x4, local copies, waits for them, and re-layouts  3.58 us

profile of v2, /device:TPU:1, one launch (start us, length us, event | category | flops | bytes accessed | tf_op | source)
XLA Modules:
  0.0 176.8 jit_solution(15807157056347609804)
XLA Ops:
  1.3 0.9 multiply_multiply_fusion
  2.2 1.0 fusion
  3.2 0.8 concatenate.3.rows_in
  4.0 169.2 %fused_step.1 = (f32[128,3072]{1,0:T(8,128)}, f32[192,768]{1,0:T(8,128)}) custom-call(bf16[128,3072]{1,0:T(8,128)(2,1)} %bitcast.16, bf16[128,3072]{1,0:T(8,128)(2,1)} %bitcast.17, f32[8,3072]{1,0:T(8,128)} %concatenate.3.rows_in, bf16[3072,768]{1,0:T(8,128)(2,1)} %up_in.1, bf16[768,3072]{1,0:T(8,128)(2,1)} %down_in.1, bf16[192,768]{1,0:T(8,128)(2,1)} %off_in.1), custom_call_target="tpu_custom_call" | custom-call | flops 24159191040 | bytes 41943040 | tf_op jit(solution)/shard_map/fused_step/pallas_call | solution.py:495
  173.2 0.0 copy-start
  173.2 2.8 %copy.12 = f32[1,128,3072]{2,1,0:T(8,128)} copy(f32[1,128,3072]{2,1,0:T(8,128)} %bitcast.15) | data formatting | bytes 3145728
  175.9 0.0 copy-done
  175.9 0.8 copy.13
Async XLA Ops:
  173.2 2.8 %copy-start = (f32[192,768]{1,0:T(8,128)S(1)}, f32[192,768]{1,0:T(8,128)}, u32[]{:S(2)}) copy-start(f32[192,768]{1,0:T(8,128)} %get-tuple-element.13) | copy-start | bytes 1769476

commit v3 on v2

--- a/solution.py
+++ b/solution.py
@@ -16,7 +16,7 @@
 HH = 768
 NT = (((1,), (1,)), ((), ()))
 NN = (((1,), (0,)), ((), ()))
-N_MSG = 144
+N_MSG = 160
 
 
 def gelu_both(value):
@@ -41,9 +41,9 @@
 
 
 def kernel(
-    st_in, adj_in, rows_in, up_in, down_in, off_in,
+    st_hbm, adj_hbm, rows_hbm, up_in, down_in, off_in,
     rate_out, og_out,
-    modb, gatb, upb, downb, ofs, actb, slp, ghb, sact, swgt, sopp, sun, sai, aid,
+    st_in, adj_in, rows_in, modb, gatb, upb, downb, ofs, actb, slp, ghb, sact, swgt, sopp, sun, sai, aid,
     vA, vB, vL, vR, jA, jB, jL, jR, zA, zB, zL, zR, yA, yB, yL, yR, ysum, yr, zsum, zr,
     ss, rs, ls,
 ):
@@ -92,18 +92,19 @@
         copy.start()
         return copy
 
-    l_up = local(0, up_in, upb.at[yh])
-    l_off = local(1, off_in, ofs.at[yh, c, yl, z])
-    l_down = local(2, down_in, downb.at[yh])
-
     barrier = pltpu.get_barrier_semaphore()
     peers = (right, left, zright, zleft, zfar, yright, yleft, yfar, sib)
     for peer in peers:
         pl.semaphore_signal(barrier, inc=1, device_id=peer, device_id_type=MESH)
+    l_pre = [local(0, st_hbm, st_in), local(1, adj_hbm, adj_in), local(2, rows_hbm, rows_in)]
+    l_up = local(3, up_in, upb.at[yh])
+    l_off = local(4, off_in, ofs.at[yh, c, yl, z])
+    l_down = local(5, down_in, downb.at[yh])
     pl.semaphore_wait(barrier, len(peers))
 
     lo, hi = pl.ds(0, T // 2), pl.ds(T // 2, T // 2)
-    E0, E1 = pl.ds(0, 384), pl.ds(384, 384)
+    E0, E1 = pl.ds(0, 512), pl.ds(512, 256)
+    G0, G1 = pl.ds(0, 384), pl.ds(384, 384)
 
     def ring_start(src, own, nxt, prv):
         return [send(src, own, nxt), send(src, own, prv)]
@@ -126,33 +127,47 @@
         b = send(buf.at[2, hi, cols], buf.at[3, hi, cols], left)
         return [a, b]
 
-    def piece(buf, zz, size, half=None):
-        first = (zz * 2 + c) * size
+    def tok_start(buf):
+        def one(rows, slot, device):
+            return send(buf.at[0, rows], buf.at[slot, rows], device)
+
+        return [one(lo, 1, right), one(hi, 2, left), one(hi, 1, right), one(lo, 2, left)]
+
+    def tok_mid(buf, first):
+        first[0].wait_recv()
+        a = send(buf.at[1, lo], buf.at[3, lo], right)
+        first[1].wait_recv()
+        b = send(buf.at[2, hi], buf.at[3, hi], left)
+        return [a, b]
+
+    def piece(buf, zz, part, half=None):
+        size, k, n = part
+        first, rows = (zz * 2 + c) * size + k * (size // n), size // n
         if half is None:
-            return buf.at[oh, pl.ds(first, size)]
-        return buf.at[oh, pl.ds(first + half * (size // 2), size // 2)]
-
-    def w_start(src, buf, size):
-        r = pl.ds((z * 2 + c) * size, size)
+            return buf.at[oh, pl.ds(first, rows)]
+        return buf.at[oh, pl.ds(first + half * (rows // 2), rows // 2)]
+
+    def w_start(src, buf, part):
+        size, k, n = part
+        r = pl.ds((z * 2 + c) * size + k * (size // n), size // n)
         return send(src.at[r], buf.at[yh, r], ypair)
 
-    def w_ring(buf, size, first):
+    def w_ring(buf, part, first):
         first.wait_recv()
-        p = piece(buf, z, size)
+        p = piece(buf, z, part)
         return ring_start(p, p, zright, zleft) + [send(p, p, sib)]
 
-    def w_mid(buf, size, msgs):
-        out = ring_mid(msgs, piece(buf, z_dn, size, 0), piece(buf, z_up, size, 1), zright, zleft)
-        p, q = piece(buf, z_dn, size), piece(buf, z_up, size)
+    def w_mid(buf, part, msgs):
+        out = ring_mid(msgs, piece(buf, z_dn, part, 0), piece(buf, z_up, part, 1), zright, zleft)
+        p, q = piece(buf, z_dn, part), piece(buf, z_up, part)
         return out + [send(p, p, sib), send(q, q, sib)]
 
-    def w_end(buf, size, msgs):
+    def w_end(buf, part, msgs):
         arrived(msgs[:2])
-        p = piece(buf, z_op, size)
+        p = piece(buf, z_op, part)
         return [send(p, p, sib)]
 
-    USZ, DSZ = D // 8, HH // 8
-    ALL = pl.ds(0, D)
+    UA, UB, DP = (D // 8, 0, 2), (D // 8, 1, 2), (HH // 8, 0, 1)
 
     def oblock(yy, zz, cols, half=None):
         rows = pl.ds(0, 192) if half is None else pl.ds(96 * half, 96)
@@ -166,9 +181,9 @@
         hs = pl.ds(0, 2) if half is None else pl.ds(half, 1)
         return ofs.at[hs, c, :, zz, :, E1]
 
-    u1 = w_start(up_in, upb, USZ)
+    u1a = w_start(up_in, upb, UA)
+    oB = ring_start(off_in.at[:, E1], oblock(y, z, E1), yright, yleft)
     oA = ring_start(off_in.at[:, E0], oblock(y, z, E0), zright, zleft)
-    oB = ring_start(off_in.at[:, E1], oblock(y, z, E1), yright, yleft)
 
     def norm_of(rows):
         inputs = st_in[rows, :].astype(F32)
@@ -184,8 +199,10 @@
         modb[0, rows, :] = (normed * rows_in[3:4, :] + rows_in[2:3, :]).astype(BF)
         gatb[0, rows, :] = (adj_in[rows, :].astype(F32) * rows_in[0:1, :]).astype(BF)
 
+    for copy in l_pre:
+        copy.wait()
     loop(T // 16, prepare)
-    m1 = xg_start(modb, ALL)
+    m1 = tok_start(modb)
 
     def p_hidden(h, row0, rows, slot0):
         def body(j):
@@ -207,48 +224,48 @@
 
         loop(HH // 256, body)
 
-    l_up.wait()
-    p_hidden(yh, 0, T, 0)
-
     l_off.wait()
+    oB2 = ring_mid(oB, oblock(y_dn, z, E1, 0), oblock(y_up, z, E1, 1), yright, yleft)
+    u1b = w_start(up_in, upb, UB)
     oA2 = ring_mid(oA, oblock(y, z_dn, E0, 0), oblock(y, z_up, E0, 1), zright, zleft)
-    oB2 = ring_mid(oB, oblock(y_dn, z, E1, 0), oblock(y_up, z, E1, 1), yright, yleft)
+    u2a = w_ring(upb, UA, u1a)
+    arrived(oB2)
+    zb = zbundle(z)
+    oD = ring_start(zb, zb, zright, zleft) + [send(zb, zb, sib)]
     arrived(oA2)
     yb = ybundle(y)
     oC = ring_start(yb, yb, yright, yleft) + [send(yb, yb, sib)]
-    arrived(oB2)
-    u2 = w_ring(upb, USZ, u1)
-    zb = zbundle(z)
-    oD = ring_start(zb, zb, zright, zleft) + [send(zb, zb, sib)]
-
-    m2 = xg_mid(modb, ALL, m1)
-    g1 = xg_start(gatb, ALL)
+    l_up.wait()
+    p_hidden(yh, 0, T, 0)
+    m2 = tok_mid(modb, m1)
+    u3a = w_mid(upb, UA, u2a)
+    oD2 = ring_mid(oD, zbundle(z_dn, 0), zbundle(z_up, 1), zright, zleft)
+    zd, zu = zbundle(z_dn), zbundle(z_up)
+    oD3 = [send(zd, zd, sib), send(zu, zu, sib)]
+    u2b = w_ring(upb, UB, u1b)
+    arrived(m1[2:])
+    g1 = tok_start(gatb)
     p_hidden(yh, T, 2 * T, 1)
-    u3 = w_mid(upb, USZ, u2)
+    oC2 = ring_mid(oC, ybundle(y_dn, 0), ybundle(y_up, 1), yright, yleft)
+    yd, yu = ybundle(y_dn), ybundle(y_up)
+    oC3 = [send(yd, yd, sib), send(yu, yu, sib)]
+    d1 = w_start(down_in, downb, DP)
+    u4a = w_end(upb, UA, u3a)
+    u3b = w_mid(upb, UB, u2b)
     arrived(m2)
     p_hidden(yh, 3 * T, T, 3)
     a1 = send(actb.at[yh], sact.at[yh], sib)
-
-    oC2 = ring_mid(oC, ybundle(y_dn, 0), ybundle(y_up, 1), yright, yleft)
-    d1 = w_start(down_in, downb, DSZ)
-    yd, yu = ybundle(y_dn), ybundle(y_up)
-    oC3 = [send(yd, yd, sib), send(yu, yu, sib)]
-    oD2 = ring_mid(oD, zbundle(z_dn, 0), zbundle(z_up, 1), zright, zleft)
-    zd, zu = zbundle(z_dn), zbundle(z_up)
-    oD3 = [send(zd, zd, sib), send(zu, zu, sib)]
-    u4 = w_end(upb, USZ, u3)
-
-    g2 = xg_mid(gatb, ALL, g1)
-    arrived([u2[2], u3[2], u3[3]] + u4)
-    p_hidden(oh, 0, 4 * T, 0)
-    a2 = send(actb.at[oh], sact.at[oh], sib)
+    arrived(oD2)
+    zo = zbundle(z_op)
+    oD4 = [send(zo, zo, sib)]
+    u4b = w_end(upb, UB, u3b)
     arrived(oC2)
     yo = ybundle(y_op)
     oC4 = [send(yo, yo, sib)]
-    arrived(oD2)
-    zo = zbundle(z_op)
-    oD4 = [send(zo, zo, sib)]
-    d2 = w_ring(downb, DSZ, d1)
+    g2 = tok_mid(gatb, g1)
+    arrived([u2a[2], u3a[2], u3a[3], u2b[2], u3b[2], u3b[3]] + u4a + u4b)
+    p_hidden(oh, 0, 4 * T, 0)
+    a2 = send(actb.at[oh], sact.at[oh], sib)
     arrived([oC[2], oD[2]] + oC3 + oC4 + oD3 + oD4)
 
     def sum_chunk(src, wt, q, k):
@@ -325,30 +342,29 @@
 
     sent(m1 + m2)
     f0, n0 = gap_calc(0)
-    l_down.wait()
-    p_gh(yh, 0, T, 0)
     f1, n1 = gap_calc(1)
     b0 = gap_aided(0, f0)
-    p_gh(yh, T, 2 * T, 1)
-    arrived(g2)
-    p_gh(yh, 3 * T, T, 3)
+    f2, n2 = gap_calc(2)
     b1 = gap_aided(1, f1)
-    f2, n2 = gap_calc(2)
     w1 = [weigh(0, n0, b0)]
+    d2 = w_ring(downb, DP, d1)
     f3, n3 = gap_calc(3)
     b2 = gap_aided(2, f2)
     w1.append(weigh(1, n1, b1))
-    d3 = w_mid(downb, DSZ, d2)
+    l_down.wait()
+    arrived(g1[2:] + g2)
+    p_gh(yh, 0, 4 * T, 0)
     b3 = gap_aided(3, f3)
     w2 = [xg_mid(modb, ccols(0), w1[0])]
     w1.append(weigh(2, n2, b2))
+    d3 = w_mid(downb, DP, d2)
     w2.append(xg_mid(modb, ccols(1), w1[1]))
     w1.append(weigh(3, n3, b3))
-    d4 = w_end(downb, DSZ, d3)
+    d4 = w_end(downb, DP, d3)
+    sent(f0 + f1 + f2 + f3 + n0 + n1 + n2 + n3 + b0 + b1 + b2 + b3)
     arrived([d2[2], d3[2], d3[3]] + d4)
     p_gh(oh, 0, 4 * T, 0)
     w2.append(xg_mid(modb, ccols(2), w1[2]))
-    sent(f0 + f1 + f2 + f3 + n0 + n1 + n2 + n3 + b0 + b1 + b2 + b3)
 
     def adj_calc(q):
         wt = [upb[h, q * 768 : q * 768 + 768, :] for h in range(2)]
@@ -367,12 +383,14 @@
     w2.append(xg_mid(modb, ccols(3), w1[3]))
     arrived(w2[0] + w2[1])
     s0 = to_sib(0)
+    jf = [send_far(pl.ds(0, 1536), jA, jB)]
+    jn = [send_near(pl.ds(0, 1536), jL, jR)]
     adj_calc(2)
-    adj_calc(3)
-    jf = [send_far(pl.ds(0, 1536), jA, jB), send_far(pl.ds(1536, 1536), jA, jB)]
-    jn = [send_near(pl.ds(0, 1536), jL, jR), send_near(pl.ds(1536, 1536), jL, jR)]
     arrived(w2[2] + w2[3])
     s1 = to_sib(1)
+    adj_calc(3)
+    jf.append(send_far(pl.ds(1536, 1536), jA, jB))
+    jn.append(send_near(pl.ds(1536, 1536), jL, jR))
 
     sent(oA + oA2 + oB + oB2 + oC + oC2 + oC3 + oC4 + oD + oD2 + oD3 + oD4)
     arrived([a1, a2, s0, s1])
@@ -388,10 +406,10 @@
     zpA, zpB = z_op // 2, z // 2
 
     def gy(yy, zs):
-        return ofs.at[yy // 2, c, yy % 2, zs, :, E1]
+        return ofs.at[yy // 2, c, yy % 2, zs, :, G1]
 
     def gz(h, zz):
-        return ofs.at[h, c, :, zz, :, E0]
+        return ofs.at[h, c, :, zz, :, G0]
 
     Z01, Z23 = pl.ds(0, 2), pl.ds(2, 2)
     g_tile(oh, yl, zpA)
@@ -409,14 +427,14 @@
 
     def add_y(yy, z0, extra):
         def body(k):
-            ref = ofs.at[yy // 2, c, yy % 2, z0 + k, :, E1]
+            ref = ofs.at[yy // 2, c, yy % 2, z0 + k, :, G1]
             ref[...] = (ref[...].astype(F32) + extra[k].astype(F32)).astype(BF)
 
         loop(2, body)
 
     def add_z(h, zz, extra):
         def body(k):
-            ref = ofs.at[h, c, k, zz, :, E0]
+            ref = ofs.at[h, c, k, zz, :, G0]
             ref[...] = (ref[...].astype(F32) + extra[k].astype(F32)).astype(BF)
 
         loop(2, body)
@@ -442,7 +460,7 @@
     arrived(ey2 + ey3)
 
     def y_total(zz):
-        return ofs[yh, c, yl, zz, :, E1].astype(F32) + yL[zz].astype(F32) + yR[zz].astype(F32)
+        return ofs[yh, c, yl, zz, :, G1].astype(F32) + yL[zz].astype(F32) + yR[zz].astype(F32)
 
     ez4 = []
     for k, (zz, target) in enumerate(((z_op, zfar), (z_up, zright), (z_dn, zleft))):
@@ -452,7 +470,7 @@
 
     def z_total(yy):
         h, k = yy // 2, yy % 2
-        return ofs[h, c, k, z, :, E0].astype(F32) + zL[h, k].astype(F32) + zR[h, k].astype(F32)
+        return ofs[h, c, k, z, :, G0].astype(F32) + zL[h, k].astype(F32) + zR[h, k].astype(F32)
 
     ey4 = []
     for k, (yy, target) in enumerate(((y_op, yfar), (y_up, yright), (y_dn, yleft))):
@@ -473,15 +491,15 @@
 
     loop(T // 16, finish)
 
-    og_out[:, E1] = y_total(z)
-    og_out[:, E0] = z_total(y)
+    og_out[:, G1] = y_total(z)
+    og_out[:, G0] = z_total(y)
     arrived(ez4)
-    og_out[:, E1] = (
-        og_out[:, E1] + zr[0].astype(F32) + zr[1].astype(F32) + zr[2].astype(F32)
+    og_out[:, G1] = (
+        og_out[:, G1] + zr[0].astype(F32) + zr[1].astype(F32) + zr[2].astype(F32)
     ) * (1.0 / 128.0)
     arrived(ey4)
-    og_out[:, E0] = (
-        og_out[:, E0] + yr[0].astype(F32) + yr[1].astype(F32) + yr[2].astype(F32)
+    og_out[:, G0] = (
+        og_out[:, G0] + yr[0].astype(F32) + yr[1].astype(F32) + yr[2].astype(F32)
     ) * (1.0 / 128.0)
     for m in list(unsent.values()):
         m.wait_send()
@@ -498,9 +516,10 @@
             jax.ShapeDtypeStruct((T, D), F32),
             jax.ShapeDtypeStruct((192, HH), F32),
         ),
-        in_specs=[vmem, vmem, vmem, hbm, hbm, hbm],
+        in_specs=[hbm] * 6,
         out_specs=(vmem, vmem),
         scratch_shapes=[
+            V((T, D), BF), V((T, D), BF), V((8, D), F32),
             V((4, T, D), BF), V((4, T, D), BF),
             V((2, D, HH), BF), V((2, HH, D), BF),
             V((2, 2, 2, 4, 192, HH), BF),
@@ -518,7 +537,7 @@
             V((3, 192, 384), BF), V((3, 192, 384), BF),
             pltpu.SemaphoreType.DMA((N_MSG,)),
             pltpu.SemaphoreType.DMA((N_MSG,)),
-            pltpu.SemaphoreType.DMA((3,)),
+            pltpu.SemaphoreType.DMA((6,)),
         ],
         compiler_params=pltpu.CompilerParams(
             collective_id=0, has_side_effects=True, vmem_limit_bytes=64 << 20
@@ -535,8 +554,11 @@
     shift, scale, gate = mods[0:1], mods[1:2], mods[2:3]
     timing = (index.astype(F32) + 1.0) / (step_count + 1.0)
     variance = 2.0 * (1.0 - timing) / timing
-    rows = jnp.concatenate(
-        [gate, 2.0 / variance * gate * gate, shift, 1.0 + scale] + [gate] * 4, axis=0
+    which = lax.broadcasted_iota(jnp.int32, (8, D), 0)
+    rows = jnp.where(
+        which == 0,
+        gate,
+        jnp.where(which == 1, 2.0 / variance * gate * gate, jnp.where(which == 2, shift, 1.0 + scale)),
     )
     rate, offset_grad = fused(states[0], adjoint[0], rows, up, down, offset)
     return rate[None], offset_grad

time: 177 us -> 162 us (0.915)
  Pallas kernels: 169 us -> 154 us
    pallas_call x1, Pallas kernels: 169 us -> 154 us  [fused(): pl.pallas_call(kernel, out_shape=(jax.ShapeDtypeStruct((T, D), F32), jax....]
where the time goes in v3:
time: 162 us; the launch traced here: 161 us
  Pallas kernels  154 us (95%)
  local copies, waits for them, and re-layouts  3.58 us (2%)
  other arithmetic  1.77 us (1%)
    pallas_call x1, Pallas kernels, fused(): pl.pallas_call(kernel, out_shape=(jax.ShapeDtypeStruct((T, D), F32), jax....  154 us
    unnamed x4, local copies, waits for them, and re-layouts  3.58 us

profile of v3, /device:TPU:1, one launch (start us, length us, event | category | flops | bytes accessed | tf_op | source)
XLA Modules:
  0.0 161.0 jit_solution(7291824234661249616)
XLA Ops:
  1.4 1.0 constant_dynamic-slice_fusion.1
  2.4 0.7 select_select_fusion.rows_hbm
  3.1 154.3 %fused_step.1 = (f32[128,3072]{1,0:T(8,128)}, f32[192,768]{1,0:T(8,128)}) custom-call(bf16[128,3072]{1,0:T(8,128)(2,1)} %bitcast.16, bf16[128,3072]{1,0:T(8,128)(2,1)} %bitcast.17, f32[8,3072]{1,0:T(8,128)} %select_select_fusion.rows_hbm, bf16[3072,768]{1,0:T(8,128)(2,1)} %up_in.1, bf16[768,3072]{1,0:T(8,128)(2,1)} %down_in.1, bf16[192,768]{1,0:T(8,128)(2,1)} %off_in.1), custom_call_target="tpu_custom_call" | custom-call | flops 24159191040 | bytes 41943040 | tf_op jit(solution)/shard_map/fused_step/pallas_call | solution.py:513
  157.4 0.0 copy-start
  157.4 2.8 %copy.12 = f32[1,128,3072]{2,1,0:T(8,128)} copy(f32[1,128,3072]{2,1,0:T(8,128)} %bitcast.11) | data formatting | bytes 3145728
  160.2 0.0 copy-done
  160.2 0.8 copy.13
  (3 shorter events, 0.0 us)
Async XLA Ops:
  157.4 2.8 %copy-start = (f32[192,768]{1,0:T(8,128)S(1)}, f32[192,768]{1,0:T(8,128)}, u32[]{:S(2)}) copy-start(f32[192,768]{1,0:T(8,128)} %get-tuple-element.14) | copy-start | bytes 1769476
